TPU v7x, 512 devices: a whole 4x4x16 slice. The times are simulated.
512 devices in a mesh: expert: 32 (over z, core), helper: 4 (over y), dp: 4 (over x).
Axes of the slice: x: 4, y: 4, z: 16, core: 2. Of those that a mesh axis runs over, the one named last changes fastest.
Arguments:
- inputs: bfloat16 [1536, 2880], P(('expert', 'dp')), may hold values from -6 to 6
- cotangent: bfloat16 [1536, 2880], P(('expert', 'dp')), may hold values from -6 to 6
- expert_ids: int32 [1536, 4], P(('expert', 'dp')), may hold values from 0 to 31, all different within a row; in each aligned block of 12 rows (0 to 11, 12 to 23, ...) at most 2 rows name the same one
- gate_values: float32 [1536, 4], P(('expert', 'dp')), may hold values from 0.1 to 1
- w_gate: bfloat16 [32, 2880, 2048], P('expert', None, ('helper', 'dp')), may hold values from -0.109375 to 0.109375
- w_up: bfloat16 [32, 2880, 2048], P('expert', None, ('helper', 'dp')), may hold values from -0.109375 to 0.109375
- w_down: bfloat16 [32, 2048, 2880], P('expert', ('helper', 'dp')), may hold values from -0.125 to 0.125
Outputs:
- grad_inputs: bfloat16 [1536, 2880], P(('expert', 'dp'), 'helper')
- grad_w_gate: bfloat16 [32, 2880, 2048], P('expert', None, ('helper', 'dp'))
- grad_w_up: bfloat16 [32, 2880, 2048], P('expert', None, ('helper', 'dp'))
- grad_w_down: bfloat16 [32, 2048, 2880], P('expert', ('helper', 'dp'))
Inputs may be any that keep to these rules, and one draw needn't show every extreme that they name: `expert_ids`: each token names 4 different experts. Within each aligned block of 12 rows (the tokens of one token shard) no expert is named by more than 2 rows, a bound that some block reaches.
All inputs are finite; a program needn't handle non-finite values.
Results may differ from a plain program's by a relative error of at most 0.0064.
Values may be sent and summed in bfloat16 or wider, within the bound.
A program may use at most 128 MiB of HBM per device.

v0:
```python
import jax
import jax.numpy as jnp
from jax import lax
from jax.sharding import PartitionSpec as P

CAP = 2


def slot_tables(expert_ids, gate_values, experts):
    shard_rows, top_count = expert_ids.shape
    flat_ids = expert_ids.reshape(shard_rows * top_count)
    onehot = (flat_ids[:, None] == jnp.arange(experts, dtype=jnp.int32)[None, :]).astype(jnp.int32)
    before = jnp.cumsum(onehot, axis=0) - onehot
    slot_index = flat_ids * CAP + jnp.sum(before * onehot, axis=1)
    owner_row = jnp.arange(shard_rows * top_count, dtype=jnp.int32) // top_count
    table_tok = jnp.zeros((experts * CAP,), jnp.int32).at[slot_index].set(owner_row)
    table_gate = (
        jnp.zeros((experts * CAP,), jnp.float32)
        .at[slot_index]
        .set(gate_values.reshape(shard_rows * top_count))
    )
    return (slot_index, table_tok, table_gate)


def pair_total(summed, slot_index, shard_rows, top_count):
    per_pair = summed[slot_index].reshape(shard_rows, top_count, summed.shape[1])
    return jnp.sum(per_pair, axis=1)


def local(inputs, cotangent, expert_ids, gate_values, w_gate, w_up, w_down):
    shard_rows, model_width = inputs.shape
    top_count = expert_ids.shape[1]
    n_expert = lax.axis_size("expert")
    n_data = lax.axis_size("dp")
    local_count = w_gate.shape[0]
    experts = local_count * n_expert
    slot_rows = local_count * CAP
    sources = n_expert * n_data
    slot_index, table_tok, table_gate = slot_tables(expert_ids, gate_values, experts)
    send_rows = inputs[table_tok]
    send_cot = (table_gate[:, None] * cotangent[table_tok].astype(jnp.float32)).astype(jnp.bfloat16)
    wide_shape = (n_expert, n_data, slot_rows, model_width)
    spread_rows = jnp.broadcast_to(
        send_rows.reshape(n_expert, 1, slot_rows, model_width), wide_shape
    )
    spread_cot = jnp.broadcast_to(send_cot.reshape(n_expert, 1, slot_rows, model_width), wide_shape)
    arrived_rows, arrived_cot = (
        lax.all_to_all(
            spread_rows.reshape(sources * slot_rows, model_width),
            ("expert", "dp"),
            split_axis=0,
            concat_axis=0,
            tiled=True,
        ),
        lax.all_to_all(
            spread_cot.reshape(sources * slot_rows, model_width),
            ("expert", "dp"),
            split_axis=0,
            concat_axis=0,
            tiled=True,
        ),
    )
    expert_rows = arrived_rows.reshape(sources, local_count, CAP, model_width)
    expert_cot = arrived_cot.reshape(sources, local_count, CAP, model_width)
    gate_pre = jnp.einsum("secd,edf->secf", expert_rows, w_gate, preferred_element_type=jnp.float32)
    up_pre = jnp.einsum("secd,edf->secf", expert_rows, w_up, preferred_element_type=jnp.float32)
    sigmoid_gate = jax.nn.sigmoid(1.702 * gate_pre)
    activated = gate_pre * sigmoid_gate
    hidden = ((up_pre + 1.0) * activated).astype(jnp.bfloat16)
    d_hidden = jnp.einsum("secd,efd->secf", expert_cot, w_down, preferred_element_type=jnp.float32)
    d_up = (d_hidden * activated).astype(jnp.bfloat16)
    slope = sigmoid_gate + 1.702 * gate_pre * sigmoid_gate * (1.0 - sigmoid_gate)
    d_gate = (d_hidden * (up_pre + 1.0) * slope).astype(jnp.bfloat16)
    grad_down = jnp.einsum(
        "secf,secd->efd", hidden, expert_cot, preferred_element_type=jnp.float32
    ).astype(jnp.bfloat16)
    grad_up = jnp.einsum(
        "secd,secf->edf", expert_rows, d_up, preferred_element_type=jnp.float32
    ).astype(jnp.bfloat16)
    grad_gate = jnp.einsum(
        "secd,secf->edf", expert_rows, d_gate, preferred_element_type=jnp.float32
    ).astype(jnp.bfloat16)
    partial_value = jnp.einsum("secf,edf->secd", d_up, w_up, preferred_element_type=jnp.float32)
    partial_value = (
        partial_value
        + jnp.einsum("secf,edf->secd", d_gate, w_gate, preferred_element_type=jnp.float32)
    ).astype(jnp.bfloat16)
    returned = lax.all_to_all(
        partial_value.reshape(sources * slot_rows, model_width),
        ("expert", "dp"),
        split_axis=0,
        concat_axis=0,
        tiled=True,
    )
    summed = jnp.sum(
        returned.reshape(n_expert, n_data, slot_rows, model_width).astype(jnp.float32), axis=1
    )
    token_sum = pair_total(
        summed.reshape(experts * CAP, model_width), slot_index, shard_rows, top_count
    )
    grad_inputs = lax.psum_scatter(token_sum, "helper", scatter_dimension=1, tiled=True).astype(
        jnp.bfloat16
    )
    return (grad_inputs, grad_gate, grad_up, grad_down)


def solution(mesh):
    in_specs = (
        P(("expert", "dp"), None),
        P(("expert", "dp"), None),
        P(("expert", "dp"), None),
        P(("expert", "dp"), None),
        P("expert", None, ("helper", "dp")),
        P("expert", None, ("helper", "dp")),
        P("expert", ("helper", "dp"), None),
    )
    out_specs = (
        P(("expert", "dp"), "helper"),
        P("expert", None, ("helper", "dp")),
        P("expert", None, ("helper", "dp")),
        P("expert", ("helper", "dp"), None),
    )
    return jax.shard_map(local, mesh=mesh, in_specs=in_specs, out_specs=out_specs, check_vma=False)
```

profile of v0, /device:TPU:1, one launch (start us, length us, event | category | flops | bytes accessed | tf_op | source)
XLA Modules:
  0.0 329.7 jit_solution(12248644198189988206)
XLA Ops:
  7.2 0.8 broadcast_multiply_fusion
  8.0 0.8 copy.23
  9.4 0.7 scatter_custom_fusion.1
  10.1 0.8 gather_fusion.1
  11.1 1.9 broadcast_in_dim.28
  13.0 20.5 %all-to-all-start.1 = ((bf16[128,2,2880]{2,1,0:T(2,128)(2,1)}), bf16[128,2,2880]{2,1,0:T(2,128)(2,1)S(1)}, u32[]{:S(2)}, u32[]{:S(2)}) async-start(bf16[128,2,2880]{2,1,0:T(2,128)(2,1)} %bitcast.95), calls=%async_computation.1 | async-start | bytes 3014656 | tf_op jit(solution)/shard_map/all_to_all | solution.py:48
  33.7 0.7 scatter_custom_fusion
  34.6 0.8 gather_fusion
  35.4 0.4 reshape.145
  36.1 72.1 %all-to-all-done.1 = bf16[128,2,2880]{2,1,0:T(2,128)(2,1)S(1)} async-done(((bf16[128,2,2880]{2,1,0:T(2,128)(2,1)}), bf16[128,2,2880]{2,1,0:T(2,128)(2,1)S(1)}, u32[]{:S(2)}, u32[]{:S(2)}) %all-to-all-start.1) | async-done | bytes 1474592 | tf_op jit(solution)/shard_map/all_to_all | solution.py:48
  108.2 1.9 broadcast_in_dim.12
  110.1 7.8 %all-to-all-start = ((bf16[128,2,2880]{2,1,0:T(2,128)(2,1)}), bf16[128,2,2880]{2,1,0:T(2,128)(2,1)}, u32[]{:S(2)}, u32[]{:S(2)}) async-start(bf16[128,2,2880]{2,1,0:T(2,128)(2,1)} %bitcast.96), calls=%async_computation | async-start | bytes 3014656 | tf_op jit(solution)/shard_map/all_to_all | solution.py:55
  117.9 3.9 %copy.26 = bf16[128,2,2880]{0,2,1:T(8,128)(2,1)S(1)} copy(bf16[128,2,2880]{2,1,0:T(2,128)(2,1)} %copy-done.3) | data formatting | bytes 2949120 | tf_op jit(solution)/shard_map/all_to_all | solution.py:48
  121.8 0.6 convolution_bitcast_fusion.3
  122.4 0.6 fusion.7
  123.1 69.1 %all-to-all-done = bf16[128,2,2880]{2,1,0:T(2,128)(2,1)} async-done(((bf16[128,2,2880]{2,1,0:T(2,128)(2,1)}), bf16[128,2,2880]{2,1,0:T(2,128)(2,1)}, u32[]{:S(2)}, u32[]{:S(2)}) %all-to-all-start) | async-done | bytes 1474592 | tf_op jit(solution)/shard_map/all_to_all | solution.py:55
  192.2 4.9 %copy.25 = bf16[128,2,2880]{0,2,1:T(8,128)(2,1)} copy(bf16[128,2,2880]{2,1,0:T(2,128)(2,1)} %all-to-all-done) | data formatting | bytes 2949120 | tf_op jit(solution)/shard_map/all_to_all | solution.py:55
  197.1 2.2 multiply_convert_fusion.2
  199.3 0.5 fusion.9
  199.9 1.7 fusion
  201.6 5.0 %copy.28 = bf16[128,2,2880]{2,1,0:T(2,128)(2,1)} copy(bf16[128,2,2880]{0,2,1:T(8,128)(2,1)} %fusion) | data formatting | bytes 2949120 | tf_op jit(solution)/shard_map/convert_element_type | solution.py:87
  206.5 7.8 %all-to-all-start.2 = ((bf16[128,2,2880]{2,1,0:T(2,128)(2,1)}), bf16[128,2,2880]{2,1,0:T(2,128)(2,1)}, u32[]{:S(2)}, u32[]{:S(2)}) async-start(bf16[128,2,2880]{2,1,0:T(2,128)(2,1)} %copy.28), calls=%async_computation.2 | async-start | bytes 3014656 | tf_op jit(solution)/shard_map/all_to_all | solution.py:88
  214.4 1.4 fusion.6
  215.8 72.9 %all-to-all-done.2 = bf16[128,2,2880]{2,1,0:T(2,128)(2,1)} async-done(((bf16[128,2,2880]{2,1,0:T(2,128)(2,1)}), bf16[128,2,2880]{2,1,0:T(2,128)(2,1)}, u32[]{:S(2)}, u32[]{:S(2)}) %all-to-all-start.2) | async-done | bytes 1474592 | tf_op jit(solution)/shard_map/all_to_all | solution.py:88
  288.7 4.1 %convert_reduce_fusion = f32[32,2,2880]{2,1,0:T(2,128)} fusion(bf16[128,2,2880]{2,1,0:T(2,128)(2,1)} %all-to-all-done.2), kind=kLoop, calls=%fused_computation.16 | loop fusion | flops 1290240 | bytes 2211840 | tf_op jit(solution)/shard_map/reduce_sum | solution.py:95
  292.7 1.6 reshape.142
  294.4 0.8 gather_fusion.2
  295.7 1.6 copy.32
  297.4 1.4 fusion.5
  298.8 1.4 fusion.4
  300.2 20.9 %reduce-scatter.4.cloned.1.call-done = f32[720,12]{1,0:T(8,128)} async-done(((f32[2880,12]{1,0:T(8,128)}), f32[720,12]{1,0:T(8,128)}) %reduce-scatter.4.cloned.1.call-update) | async-done | bytes 34576
  321.1 1.8 copy.33
  (46 shorter events, 2.1 us)
Async XLA Ops:
  7.2 115.3 %copy-start = (bf16[1,2880,128]{2,1,0:T(8,128)(2,1)S(1)}, bf16[1,2880,128]{2,1,0:T(8,128)(2,1)}, u32[]{:S(2)}) copy-start(bf16[1,2880,128]{2,1,0:T(8,128)(2,1)} %param.12) | copy-start | bytes 2211844
  7.2 2.9 copy-start.1
  13.0 20.5 %copy-start.12 = (f32[12,4]{0,1:T(4,128)S(1)}, f32[12,4]{0,1:T(4,128)}, u32[]{:S(2)}) copy-start(f32[12,4]{0,1:T(4,128)} %param.10) | copy-start | bytes 580
  13.0 21.6 %copy-start.2 = (bf16[12,2880]{1,0:T(8,128)(2,1)S(1)}, bf16[12,2880]{1,0:T(8,128)(2,1)}, u32[]{:S(2)}) copy-start(bf16[12,2880]{1,0:T(8,128)(2,1)} %param.8) | copy-start | bytes 207364
  13.0 95.2 %all-to-all-start.1 = ((bf16[128,2,2880]{2,1,0:T(2,128)(2,1)}), bf16[128,2,2880]{2,1,0:T(2,128)(2,1)S(1)}, u32[]{:S(2)}, u32[]{:S(2)}) async-start(bf16[128,2,2880]{2,1,0:T(2,128)(2,1)} %bitcast.95), calls=%async_computation.1 | async-start | bytes 3014656 | tf_op jit(solution)/shard_map/all_to_all | solution.py:48
  108.2 1.9 copy-start.3
  110.1 82.1 %all-to-all-start = ((bf16[128,2,2880]{2,1,0:T(2,128)(2,1)}), bf16[128,2,2880]{2,1,0:T(2,128)(2,1)}, u32[]{:S(2)}, u32[]{:S(2)}) async-start(bf16[128,2,2880]{2,1,0:T(2,128)(2,1)} %bitcast.96), calls=%async_computation | async-start | bytes 3014656 | tf_op jit(solution)/shard_map/all_to_all | solution.py:55
  117.9 3.9 %copy-start.5 = (bf16[1,2880,128]{2,1,0:T(8,128)(2,1)S(1)}, bf16[1,2880,128]{2,1,0:T(8,128)(2,1)}, u32[]{:S(2)}) copy-start(bf16[1,2880,128]{2,1,0:T(8,128)(2,1)} %param.11) | copy-start | bytes 2211844
  122.4 74.6 %copy-start.6 = (f32[128,1,2,128]{3,0,2,1:T(8,128)}, f32[128,1,2,128]{3,0,2,1:T(8,128)S(1)}, u32[]{:S(2)}) copy-start(f32[128,1,2,128]{3,0,2,1:T(8,128)S(1)} %convolution_bitcast_fusion.3) | copy-start | bytes 393220
  123.1 74.0 %copy-start.8 = (f32[128,1,2,128]{3,0,2,1:T(8,128)}, f32[128,1,2,128]{3,0,2,1:T(8,128)S(1)}, u32[]{:S(2)}) copy-start(f32[128,1,2,128]{3,0,2,1:T(8,128)S(1)} %fusion.7) | copy-start | bytes 393220
  199.3 0.6 copy-start.10
  206.5 82.1 %all-to-all-start.2 = ((bf16[128,2,2880]{2,1,0:T(2,128)(2,1)}), bf16[128,2,2880]{2,1,0:T(2,128)(2,1)}, u32[]{:S(2)}, u32[]{:S(2)}) async-start(bf16[128,2,2880]{2,1,0:T(2,128)(2,1)} %copy.28), calls=%async_computation.2 | async-start | bytes 3014656 | tf_op jit(solution)/shard_map/all_to_all | solution.py:88
  214.3 106.8 %reduce-scatter.4.cloned.1.call-start = ((), (), s32[]{:S(2)}) async-start(), calls=%async_computation.4 | async-start | bytes 1843200
  295.7 1.7 copy-start.11
  297.3 1.4 copy-start.4
  297.3 1.4 copy-start.7
  297.3 1.4 copy-start.9
Sparse Core Ops, SparseCore 0:
  297.4 23.6 reduce-scatter.3
where the time goes:
time: 331 us; the launch traced here: 330 us
  waiting for transfers between devices  235 us (71%)
  starting transfers between devices  36.1 us (11%)
  local copies, waits for them, and re-layouts  28.5 us (9%)
  between operations  14.4 us (4%)
  matrix products  9.85 us (3%)
  other arithmetic  5.87 us (2%)
    all_to_all x1, waiting for transfers between devices, local(): lax.all_to_all(partial_value.reshape(sources * slot_rows, model_width), (...  72.9 us
    all_to_all x1, waiting for transfers between devices, local(): lax.all_to_all(spread_rows.reshape(sources * slot_rows, model_width), ('e...  72.1 us
    all_to_all x1, waiting for transfers between devices, local(): lax.all_to_all(spread_cot.reshape(sources * slot_rows, model_width), ('ex...  69.1 us
    unnamed x2, waiting for transfers between devices  20.9 us
    all_to_all x1, starting transfers between devices, local(): lax.all_to_all(spread_rows.reshape(sources * slot_rows, model_width), ('e...  20.5 us
    all_to_all x1, starting transfers between devices, local(): lax.all_to_all(spread_cot.reshape(sources * slot_rows, model_width), ('ex...  7.78 us
    all_to_all x1, starting transfers between devices, local(): lax.all_to_all(partial_value.reshape(sources * slot_rows, model_width), (...  7.76 us
  transfers between devices with their start and end apart: 4, of which 4 were waited for; matrix products, arithmetic and copies ran while one was open for 4% of the time, Pallas kernels for 0%

commit v1 on v0

v1 whole, which is shorter than its diff:
```python
import functools

import jax
import jax.numpy as jnp
from jax import lax
from jax.experimental import pallas as pl
from jax.experimental.pallas import tpu as pltpu
from jax.sharding import PartitionSpec as P

CAP = 2
MESH = pl.DeviceIdType.MESH
F32 = jnp.float32
BF16 = jnp.bfloat16
NT = (((1,), (1,)), ((), ()))
TN = (((0,), (0,)), ((), ()))
NN = (((1,), (0,)), ((), ()))


def dot(a, b, dims=NN):
    return lax.dot_general(a, b, dims, preferred_element_type=F32)


def shift(i, y):
    return (1 + y, 8 - y, -y, y - 7)[i]


def pick_shift(i, y):
    return jnp.where(i == 0, 1 + y, jnp.where(i == 1, 8 - y, jnp.where(i == 2, -y, y - 7)))


def pick(idt, gvt, z, nz, i, y, core, j):
    far = z + pick_shift(i, y)
    far = jnp.where(far < 0, far + nz, jnp.where(far >= nz, far - nz, far))
    expert = far * 2 + core
    tokens = idt.shape[1]
    hits = [(idt[k : k + 1, :] == expert) for k in range(idt.shape[0])]
    named = functools.reduce(lambda a, b: a + b, [h.astype(F32) for h in hits])
    row = lax.broadcasted_iota(jnp.int32, (tokens, tokens), 0)
    col = lax.broadcasted_iota(jnp.int32, (tokens, tokens), 1)
    before = dot(named.astype(BF16), (row < col).astype(BF16))
    chosen = jnp.where(before == j.astype(F32), named, 0.0)
    weight = functools.reduce(lambda a, b: a + b, [h.astype(F32) * gvt[k : k + 1, :] for k, h in enumerate(hits)])
    return chosen, jnp.sum(chosen * weight, axis=1, keepdims=True)


def body(cuts, nz, x_ref, c_ref, idt_ref, gvt_ref, wg_hbm, wu_hbm, wd_hbm, gi_ref, gg_hbm, gu_hbm, gd_hbm, *rest):
    parts = len(cuts)
    sb, rb, gx, gc = (rest[n * parts : (n + 1) * parts] for n in range(4))
    (wcat, wd, gg, gu, gd, stage, pu, pv, ru, rv, qu, qv, su, sv, back, ts, tr,
     zs, zr, ags, agr, rss, rsr, ts_sem, tr_sem, wsem, osem) = rest[4 * parts :]
    e = lax.axis_index("expert")
    y = lax.axis_index("helper")
    x = lax.axis_index("dp")
    ne = 2 * nz
    z = e // 2
    c = e % 2
    model = x_ref.shape[1]
    quarter = model // 4

    loads = [
        pltpu.make_async_copy(wg_hbm, wcat.at[:, 0:128], wsem.at[0]),
        pltpu.make_async_copy(wu_hbm, wcat.at[:, 128:256], wsem.at[1]),
        pltpu.make_async_copy(wd_hbm, wd, wsem.at[2]),
    ]
    for load in loads:
        load.start()

    def ring(me):
        return (me + 1 + 2 * c) % 4, (me + 3 - 2 * c) % 4, (me + 2) % 4

    xa, xb, xo = ring(x)
    ya, yb, yo = ring(y)

    barrier = pltpu.get_barrier_semaphore()

    @pl.loop(1, ne)
    def _(n):
        pl.semaphore_signal(barrier, inc=1, device_id={"expert": (e + n) % ne}, device_id_type=MESH)

    for other in (xa, xb):
        pl.semaphore_signal(barrier, inc=1, device_id={"dp": other}, device_id_type=MESH)
    for other in (ya, yb):
        pl.semaphore_signal(barrier, inc=1, device_id={"helper": other}, device_id_type=MESH)

    idt = idt_ref[...]
    gvt = gvt_ref[...]
    r = lax.broadcasted_iota(jnp.int32, (32, 1), 0)
    half = (r // 2) % 2
    chosen, gate = pick(idt, gvt, z, nz, r // 8, y, (r // 4) % 2, r % 2)
    pick_x = jnp.where(half == 0, chosen, 0.0).astype(BF16)
    pick_c = jnp.where(half == 1, chosen, 0.0).astype(BF16)
    start = 0
    for h, width in enumerate(cuts):
        rows = dot(pick_x, x_ref[:, start : start + width]) + gate * dot(pick_c, c_ref[:, start : start + width])
        for s in range(8):
            sb[h][s] = rows[4 * s : 4 * s + 4, :].astype(BF16)
        start += width

    pl.semaphore_wait(barrier, ne - 1 + 4)

    for h in range(parts):
        for i in (1, 3, 0, 2):
            to = (z + shift(i, y) + nz) % nz
            for core in range(2):
                s = 2 * i + core
                far = pltpu.make_async_remote_copy(
                    sb[h].at[s], rb[h].at[2 * i + c], zs.at[h], zr.at[h],
                    device_id={"expert": to * 2 + core}, device_id_type=MESH,
                )
                if i == 2:
                    own = (y == 0) & (c == core)

                    @pl.when(own)
                    def _():
                        pltpu.make_async_copy(sb[h].at[s], rb[h].at[2 * i + c], zr.at[h]).start()

                    @pl.when(jnp.logical_not(own))
                    def _():
                        far.start()
                else:
                    far.start()

    def wait(ref, sem):
        pltpu.make_async_copy(ref, ref, sem).wait()

    class Gather:
        def __init__(self, view, me, axis, ends, h, a, phase):
            self.view, self.me, self.axis = view, me, axis
            self.ahead, self.behind, self.opposite = ends
            self.ss = [ags.at[h, a, phase, n] for n in range(3)]
            self.rs = [agr.at[h, a, phase, n] for n in range(3)]

        def copy(self, at, n, to):
            return pltpu.make_async_remote_copy(
                self.view(at), self.view(at), self.ss[n], self.rs[n],
                device_id={self.axis: to}, device_id_type=MESH,
            )

        def start(self):
            self.copy(self.me, 0, self.ahead).start()
            self.copy(self.me, 1, self.behind).start()

        def forward(self):
            wait(self.view(self.behind), self.rs[0])
            self.copy(self.behind, 2, self.ahead).start()

        def finish(self):
            wait(self.view(self.ahead), self.rs[1])
            wait(self.view(self.opposite), self.rs[2])

        def sent(self):
            wait(self.view(self.me), self.ss[0])
            wait(self.view(self.me), self.ss[1])
            wait(self.view(self.behind), self.ss[2])

    xends, yends = (xa, xb, xo), (ya, yb, yo)
    first = [
        (Gather(lambda n, h=h: gx[h].at[n, y], x, "dp", xends, h, 0, 0),
         Gather(lambda n, h=h: gc[h].at[x, n], y, "helper", yends, h, 1, 0))
        for h in range(parts)
    ]
    second = [
        (Gather(lambda n, h=h: gx[h].at[:, n], y, "helper", yends, h, 0, 1),
         Gather(lambda n, h=h: gc[h].at[n], x, "dp", xends, h, 1, 1))
        for h in range(parts)
    ]

    def arrive(h):
        wait(rb[h], zr.at[h])
        width = cuts[h]
        for s in range(8):
            rows = rb[h][s].astype(F32)
            stage[2 * s : 2 * s + 2, 0:width] = rows[0:2]
            stage[16 + 2 * s : 18 + 2 * s, 0:width] = rows[2:4]
        gx[h][x, y] = stage[0:16, 0:width].astype(BF16)
        gc[h][x, y] = stage[16:32, 0:width].astype(BF16)
        for g in first[h]:
            g.start()

    def run(group, what):
        for g in group:
            getattr(g, what)()

    for h in range(parts):
        arrive(h)
        run(first[h], "forward")
        if h:
            run(second[h - 1], "forward")
        run(first[h], "finish")
        run(second[h], "start")

    total = 256
    pre = jnp.zeros((total, 256), F32)
    d_hidden = jnp.zeros((total, 128), F32)
    start = 0
    for h in range(parts):
        if h == parts - 1:
            run(second[h], "forward")
        run(second[h], "finish")
        if h == 0:
            for load in loads:
                load.wait()
        width = cuts[h]
        pre = pre + dot(gx[h][...].reshape(total, width), wcat[start : start + width, :])
        d_hidden = d_hidden + dot(gc[h][...].reshape(total, width), wd[start : start + width, :])
        start += width

    gate_pre = pre[:, 0:128]
    up1 = pre[:, 128:256] + 1.0
    sig = jax.nn.sigmoid(1.702 * gate_pre)
    activated = gate_pre * sig
    hidden = (up1 * activated).astype(BF16)
    d_up = (d_hidden * activated).astype(BF16)
    d_gate = (d_hidden * up1 * (sig + 1.702 * gate_pre * sig * (1.0 - sig))).astype(BF16)
    dcat = jnp.concatenate([d_gate, d_up], axis=1)

    for q in range(4):
        part = dot(dcat, wcat[quarter * q : quarter * (q + 1), :], NT)
        for n in range(4):
            pu[n, q] = part[64 * n : 64 * n + 32, :].astype(BF16)
            pv[n, q] = part[64 * n + 32 : 64 * n + 64, :].astype(BF16)

    class Scatter:
        def __init__(self, view, land, me, axis, ends, a, phase):
            self.view, self.land, self.me, self.axis = view, land, me, axis
            self.ahead, self.behind, self.opposite = ends
            self.ss = [rss.at[a, phase, n] for n in range(3)]
            self.rs = [rsr.at[a, phase, n] for n in range(3)]

        def copy(self, at, n, to):
            return pltpu.make_async_remote_copy(
                self.view(at), self.land.at[n], self.ss[n], self.rs[n],
                device_id={self.axis: to}, device_id_type=MESH,
            )

        def start(self):
            self.copy(self.opposite, 0, self.ahead).start()
            self.copy(self.behind, 1, self.behind).start()

        def forward(self):
            wait(self.land.at[0], self.rs[0])
            ref = self.view(self.ahead)
            ref[...] = (ref[...].astype(F32) + self.land[0].astype(F32)).astype(BF16)
            self.copy(self.ahead, 2, self.ahead).start()

        def finish(self):
            wait(self.land.at[1], self.rs[1])
            wait(self.land.at[2], self.rs[2])
            return self.view(self.me)[...].astype(F32) + self.land[1].astype(F32) + self.land[2].astype(F32)

        def sent(self):
            for n in range(3):
                wait(self.land.at[n], self.ss[n])

    u1 = Scatter(lambda n: pu.at[n], ru, x, "dp", xends, 0, 0)
    v1 = Scatter(lambda n: pv.at[:, n], rv, y, "helper", yends, 1, 0)
    u2 = Scatter(lambda n: qu.at[n], su, y, "helper", yends, 0, 1)
    v2 = Scatter(lambda n: qv.at[n], sv, x, "dp", xends, 1, 1)
    u1.start()
    v1.start()

    def weight_grads(h):
        begin = sum(cuts[:h])
        width = cuts[h]
        both = dot(gx[h][...].reshape(total, width), dcat, TN).astype(BF16)
        gg[begin : begin + width, :] = both[:, 0:128]
        gu[begin : begin + width, :] = both[:, 128:256]
        gd[begin : begin + width, :] = dot(gc[h][...].reshape(total, width), hidden, TN).astype(BF16)

    weight_grads(0)
    u1.forward()
    v1.forward()
    for h in range(1, parts):
        weight_grads(h)
    stores = [
        pltpu.make_async_copy(gg, gg_hbm, osem.at[0]),
        pltpu.make_async_copy(gu, gu_hbm, osem.at[1]),
        pltpu.make_async_copy(gd, gd_hbm, osem.at[2]),
    ]
    for store in stores:
        store.start()
    qu[...] = u1.finish().astype(BF16)
    u2.start()
    qv[...] = v1.finish().astype(BF16)
    v2.start()
    u2.forward()
    v2.forward()

    back[0:32, :] = u2.finish()
    back[32:64, :] = v2.finish()
    for m in range(32):
        ts[m] = back[2 * m : 2 * m + 2, :].astype(BF16)
    for plane in range(4):
        for i in range(4):
            to = (z - shift(i, plane) + nz) % nz
            for core in range(2):
                base = (plane * 4 + i) * 2
                far = pltpu.make_async_remote_copy(
                    ts.at[base + core], tr.at[base + c], ts_sem, tr_sem,
                    device_id={"expert": to * 2 + core}, device_id_type=MESH,
                )
                if shift(i, plane) == 0:

                    @pl.when(c == core)
                    def _():
                        pltpu.make_async_copy(ts.at[base + core], tr.at[base + c], tr_sem).start()

                    @pl.when(c != core)
                    def _():
                        far.start()
                else:
                    far.start()

    r = lax.broadcasted_iota(jnp.int32, (64, 1), 0)
    home, _ = pick(idt, gvt, z, nz, (r // 4) % 4, r // 16, (r // 2) % 2, r % 2)
    wait(tr, tr_sem)
    for m in range(32):
        back[2 * m : 2 * m + 2, :] = tr[m].astype(F32)
    gi_ref[...] = dot(home.astype(BF16), back[...].astype(BF16), TN).astype(BF16)

    for h in range(parts):

        @pl.when(y == 0)
        def _():
            wait(sb[h].at[0:7], zs.at[h])

        @pl.when(y != 0)
        def _():
            wait(sb[h], zs.at[h])

        run(first[h], "sent")
        run(second[h], "sent")
    for s in (u1, v1, u2, v2):
        s.sent()
    wait(ts.at[0:31], ts_sem)
    for store in stores:
        store.wait()


def local(inputs, cotangent, expert_ids, gate_values, w_gate, w_up, w_down):
    tokens, model = inputs.shape
    nz = lax.axis_size("expert") // 2
    hidden = w_gate.shape[2]
    quarter = model // 4
    cuts = (1536, model - 1536)
    vmem = pl.BlockSpec(memory_space=pltpu.VMEM)
    anywhere = pl.BlockSpec(memory_space=pl.ANY)
    scratch = [pltpu.VMEM((8, 4, w), BF16) for w in cuts]
    scratch += [pltpu.VMEM((8, 4, w), BF16) for w in cuts]
    scratch += [pltpu.VMEM((4, 4, 16, w), BF16) for w in cuts]
    scratch += [pltpu.VMEM((4, 4, 16, w), BF16) for w in cuts]
    scratch += [
        pltpu.VMEM((model, 2 * hidden), BF16),
        pltpu.VMEM((model, hidden), BF16),
        pltpu.VMEM((model, hidden), BF16),
        pltpu.VMEM((model, hidden), BF16),
        pltpu.VMEM((model, hidden), BF16),
        pltpu.VMEM((32, max(cuts)), F32),
        pltpu.VMEM((4, 4, 32, quarter), BF16),
        pltpu.VMEM((4, 4, 32, quarter), BF16),
        pltpu.VMEM((3, 4, 32, quarter), BF16),
        pltpu.VMEM((3, 4, 32, quarter), BF16),
        pltpu.VMEM((4, 32, quarter), BF16),
        pltpu.VMEM((4, 32, quarter), BF16),
        pltpu.VMEM((3, 32, quarter), BF16),
        pltpu.VMEM((3, 32, quarter), BF16),
        pltpu.VMEM((64, quarter), F32),
        pltpu.VMEM((32, 2, quarter), BF16),
        pltpu.VMEM((32, 2, quarter), BF16),
        pltpu.SemaphoreType.DMA((len(cuts),)),
        pltpu.SemaphoreType.DMA((len(cuts),)),
        pltpu.SemaphoreType.DMA((len(cuts), 2, 2, 3)),
        pltpu.SemaphoreType.DMA((len(cuts), 2, 2, 3)),
        pltpu.SemaphoreType.DMA((2, 2, 3)),
        pltpu.SemaphoreType.DMA((2, 2, 3)),
        pltpu.SemaphoreType.DMA,
        pltpu.SemaphoreType.DMA,
        pltpu.SemaphoreType.DMA((3,)),
        pltpu.SemaphoreType.DMA((3,)),
    ]
    grad = jax.ShapeDtypeStruct((model, hidden), BF16)
    gi, gg, gu, gd = pl.pallas_call(
        functools.partial(body, cuts, nz),
        out_shape=(jax.ShapeDtypeStruct((tokens, quarter), BF16), grad, grad, grad),
        in_specs=[vmem] * 4 + [anywhere] * 3,
        out_specs=(vmem, anywhere, anywhere, anywhere),
        scratch_shapes=scratch,
        compiler_params=pltpu.CompilerParams(
            collective_id=0, has_side_effects=True, vmem_limit_bytes=56 * 1024 * 1024
        ),
    )(
        inputs,
        cotangent,
        expert_ids.T,
        gate_values.T,
        w_gate[0],
        w_up[0],
        w_down[0].T,
    )
    return gi, gg[None], gu[None], gd.T[None]


def solution(mesh):
    in_specs = (
        P(("expert", "dp"), None),
        P(("expert", "dp"), None),
        P(("expert", "dp"), None),
        P(("expert", "dp"), None),
        P("expert", None, ("helper", "dp")),
        P("expert", None, ("helper", "dp")),
        P("expert", ("helper", "dp"), None),
    )
    out_specs = (
        P(("expert", "dp"), "helper"),
        P("expert", None, ("helper", "dp")),
        P("expert", None, ("helper", "dp")),
        P("expert", ("helper", "dp"), None),
    )
    return jax.shard_map(local, mesh=mesh, in_specs=in_specs, out_specs=out_specs, check_vma=False)
```

time: 331 us -> 93.7 us (0.28)
  waiting for transfers between devices: 235 us -> 0 us
  Pallas kernels: 0 us -> 87 us
  starting transfers between devices: 36.1 us -> 0 us
  local copies, waits for them, and re-layouts: 28.5 us -> 5.69 us
  between operations: 14.4 us -> 0.64 us
  matrix products: 9.85 us -> 0 us
  other arithmetic: 5.87 us -> 0 us
    all_to_all x3 -> x0, waiting for transfers between devices: 214 us -> none  [the longest x1 72.9 us: local(): lax.all_to_all(partial_value.reshape(sources * slot_rows, model_width), (...]
    pallas_call x0 -> x1, Pallas kernels: none -> 87 us  [local(): pl.pallas_call(functools.partial(body, cuts, nz), out_shape=(jax.ShapeDty...]
    all_to_all x3 -> x0, starting transfers between devices: 36.1 us -> none  [the longest x1 20.5 us: local(): lax.all_to_all(spread_rows.reshape(sources * slot_rows, model_width), ('e...]
    unnamed x2 -> x0, waiting for transfers between devices: 20.9 us -> none
    dot_general x8 -> x0, matrix products: 9.85 us -> none  [the longest x1 2.19 us: local(): jnp.einsum('secd,efd->secf', expert_cot, w_down, preferred_element_type=j...]
    all_to_all x2 -> x0, local copies, waits for them, and re-layouts: 8.79 us -> none  [the longest x1 4.86 us: local(): lax.all_to_all(spread_cot.reshape(sources * slot_rows, model_width), ('ex...]
    convert_element_type x2 -> x0, local copies, waits for them, and re-layouts: 5.32 us -> none  [the longest x1 4.96 us: local(): partial_value = (partial_value + jnp.einsum('secf,edf->secd', d_gate, w_g...]
    reduce_sum x3 -> x0, other arithmetic: 4.59 us -> none  [the longest x1 4.08 us: local(): jnp.sum(returned.reshape(n_expert, n_data, slot_rows, model_width).astype...]
  transfers between devices with their start and end apart: 4 -> 0, of which waited for: 4 -> 0; matrix products, arithmetic and copies ran while one was open for 4% -> 0% of each run, Pallas kernels for 0% -> 0%
where the time goes in v1:
time: 93.7 us; the launch traced here: 93.4 us
  Pallas kernels  87 us (93%)
  local copies, waits for them, and re-layouts  5.69 us (6%)
    pallas_call x1, Pallas kernels, local(): pl.pallas_call(functools.partial(body, cuts, nz), out_shape=(jax.ShapeDty...  87 us
    unnamed x8, local copies, waits for them, and re-layouts  5.69 us

profile of v1, /device:TPU:1, one launch (start us, length us, event | category | flops | bytes accessed | tf_op | source)
XLA Modules:
  0.0 93.4 jit_solution(1559422338068128657)
XLA Ops:
  0.6 87.0 %shard_map.102 = (bf16[12,720]{1,0:T(8,128)(2,1)}, bf16[2880,128]{1,0:T(8,128)(2,1)}, bf16[2880,128]{1,0:T(8,128)(2,1)}, bf16[2880,128]{1,0:T(8,128)(2,1)}) custom-call(bf16[12,2880]{1,0:T(8,128)(2,1)} %x_ref.1, bf16[12,2880]{1,0:T(8,128)(2,1)} %c_ref.1, s32[4,12]{1,0:T(4,128)} %bitcast.18, f32[4,12]{1,0:T(4,128)} %bitcast.19, bf16[2880,128]{1,0:T(8,128)(2,1)} %bitcast.12, ...), custom_call_target="tpu_custom_call" | custom-call | tf_op jit(solution)/shard_map/pallas_call | solution.py:382
  87.7 1.3 %copy.15 = bf16[12,720]{1,0:T(8,128)(2,1)} copy(bf16[12,720]{1,0:T(8,128)(2,1)} %get-tuple-element.16) | data formatting | bytes 34560
  89.0 0.0 copy-start.1
  89.0 2.1 %copy.16 = bf16[1,2880,128]{2,1,0:T(8,128)(2,1)} copy(bf16[1,2880,128]{2,1,0:T(8,128)(2,1)} %bitcast.17) | data formatting | bytes 1474560
  91.1 0.0 copy-done.1
  91.1 0.0 copy-start
  91.1 0.9 copy.17
  92.0 0.5 copy-done
  92.5 0.9 copy.18
Async XLA Ops:
  89.0 2.1 %copy-start.1 = (bf16[2880,128]{1,0:T(8,128)(2,1)S(1)}, bf16[2880,128]{1,0:T(8,128)(2,1)}, u32[]{:S(2)}) copy-start(bf16[2880,128]{1,0:T(8,128)(2,1)} %get-tuple-element.10) | copy-start | bytes 2211844
  91.1 1.4 %copy-start = (bf16[2880,128]{1,0:T(8,128)(2,1)S(1)}, bf16[2880,128]{1,0:T(8,128)(2,1)}, u32[]{:S(2)}) copy-start(bf16[2880,128]{1,0:T(8,128)(2,1)} %get-tuple-element.11) | copy-start | bytes 2211844

commit v2 on v1

--- a/solution.py
+++ b/solution.py
@@ -43,20 +43,45 @@
     return chosen, jnp.sum(chosen * weight, axis=1, keepdims=True)
 
 
-def body(cuts, nz, x_ref, c_ref, idt_ref, gvt_ref, wg_hbm, wu_hbm, wd_hbm, gi_ref, gg_hbm, gu_hbm, gd_hbm, *rest):
+def body(cuts, nz, x_hbm, c_hbm, idt_hbm, gvt_hbm, wg_hbm, wu_hbm, wd_hbm, gi_ref, gg_hbm, gu_hbm, gd_hbm, *rest):
     parts = len(cuts)
     sb, rb, gx, gc = (rest[n * parts : (n + 1) * parts] for n in range(4))
-    (wcat, wd, gg, gu, gd, stage, pu, pv, ru, rv, qu, qv, su, sv, back, ts, tr,
-     zs, zr, ags, agr, rss, rsr, ts_sem, tr_sem, wsem, osem) = rest[4 * parts :]
+    (x_ref, c_ref, idt_ref, gvt_ref, wcat, wd, gg, gu, gd, stage, pu, pv, ru, rv, qu, qv, su, sv, back, ts, tr,
+     zs, zr, ags, agr, rss, rsr, ts_sem, tr_sem, isem, wsem, osem) = rest[4 * parts :]
     e = lax.axis_index("expert")
     y = lax.axis_index("helper")
     x = lax.axis_index("dp")
     ne = 2 * nz
     z = e // 2
     c = e % 2
-    model = x_ref.shape[1]
+    model = x_hbm.shape[1]
     quarter = model // 4
 
+    def ring(me):
+        return (me + 1 + 2 * c) % 4, (me + 3 - 2 * c) % 4, (me + 2) % 4
+
+    xa, xb, xo = ring(x)
+    ya, yb, yo = ring(y)
+
+    barrier = pltpu.get_barrier_semaphore()
+
+    @pl.loop(1, ne)
+    def _(n):
+        pl.semaphore_signal(barrier, inc=1, device_id={"expert": (e + n) % ne}, device_id_type=MESH)
+
+    for other in (xa, xb, xo):
+        pl.semaphore_signal(barrier, inc=1, device_id={"dp": other}, device_id_type=MESH)
+    for other in (ya, yb, yo):
+        pl.semaphore_signal(barrier, inc=1, device_id={"helper": other}, device_id_type=MESH)
+
+    fetches = [
+        pltpu.make_async_copy(idt_hbm, idt_ref, isem.at[0]),
+        pltpu.make_async_copy(gvt_hbm, gvt_ref, isem.at[1]),
+        pltpu.make_async_copy(x_hbm, x_ref, isem.at[2]),
+        pltpu.make_async_copy(c_hbm, c_ref, isem.at[3]),
+    ]
+    for fetch in fetches:
+        fetch.start()
     loads = [
         pltpu.make_async_copy(wg_hbm, wcat.at[:, 0:128], wsem.at[0]),
         pltpu.make_async_copy(wu_hbm, wcat.at[:, 128:256], wsem.at[1]),
@@ -64,23 +89,8 @@
     ]
     for load in loads:
         load.start()
-
-    def ring(me):
-        return (me + 1 + 2 * c) % 4, (me + 3 - 2 * c) % 4, (me + 2) % 4
-
-    xa, xb, xo = ring(x)
-    ya, yb, yo = ring(y)
-
-    barrier = pltpu.get_barrier_semaphore()
-
-    @pl.loop(1, ne)
-    def _(n):
-        pl.semaphore_signal(barrier, inc=1, device_id={"expert": (e + n) % ne}, device_id_type=MESH)
-
-    for other in (xa, xb):
-        pl.semaphore_signal(barrier, inc=1, device_id={"dp": other}, device_id_type=MESH)
-    for other in (ya, yb):
-        pl.semaphore_signal(barrier, inc=1, device_id={"helper": other}, device_id_type=MESH)
+    for fetch in fetches:
+        fetch.wait()
 
     idt = idt_ref[...]
     gvt = gvt_ref[...]
@@ -96,7 +106,10 @@
             sb[h][s] = rows[4 * s : 4 * s + 4, :].astype(BF16)
         start += width
 
-    pl.semaphore_wait(barrier, ne - 1 + 4)
+    pl.semaphore_wait(barrier, ne - 1 + 6)
+
+    def wait(ref, sem):
+        pltpu.make_async_copy(ref, ref, sem).wait()
 
     for h in range(parts):
         for i in (1, 3, 0, 2):
@@ -120,9 +133,6 @@
                 else:
                     far.start()
 
-    def wait(ref, sem):
-        pltpu.make_async_copy(ref, ref, sem).wait()
-
     class Gather:
         def __init__(self, view, me, axis, ends, h, a, phase):
             self.view, self.me, self.axis = view, me, axis
@@ -153,15 +163,29 @@
             wait(self.view(self.me), self.ss[1])
             wait(self.view(self.behind), self.ss[2])
 
+    class Direct(Gather):
+        def start(self):
+            for n, to in enumerate((self.ahead, self.behind, self.opposite)):
+                self.copy(self.me, n, to).start()
+
+        def take(self, n):
+            wait(self.view((self.behind, self.ahead, self.opposite)[n]), self.rs[n])
+
+        def sent(self):
+            for n in range(3):
+                wait(self.view(self.me), self.ss[n])
+
     xends, yends = (xa, xb, xo), (ya, yb, yo)
     first = [
-        (Gather(lambda n, h=h: gx[h].at[n, y], x, "dp", xends, h, 0, 0),
-         Gather(lambda n, h=h: gc[h].at[x, n], y, "helper", yends, h, 1, 0))
+        (Direct(lambda n, h=h: gx[h].at[n, y], x, "dp", xends, h, 0, 4),
+         Direct(lambda n, h=h: gc[h].at[x, n], y, "helper", yends, h, 1, 4))
         for h in range(parts)
     ]
+    xroles, yroles = (x, xb, xa, xo), (y, yb, ya, yo)
     second = [
-        (Gather(lambda n, h=h: gx[h].at[:, n], y, "helper", yends, h, 0, 1),
-         Gather(lambda n, h=h: gc[h].at[n], x, "dp", xends, h, 1, 1))
+        [(Gather(lambda n, h=h, k=k: gx[h].at[xroles[k], n], y, "helper", yends, h, 0, k),
+          Gather(lambda n, h=h, k=k: gc[h].at[n, yroles[k]], x, "dp", xends, h, 1, k))
+         for k in range(4)]
         for h in range(parts)
     ]
 
@@ -174,36 +198,39 @@
             stage[16 + 2 * s : 18 + 2 * s, 0:width] = rows[2:4]
         gx[h][x, y] = stage[0:16, 0:width].astype(BF16)
         gc[h][x, y] = stage[16:32, 0:width].astype(BF16)
-        for g in first[h]:
-            g.start()
-
-    def run(group, what):
+        run(first[h], "start")
+        run(second[h][0], "start")
+
+    def run(group, what, *args):
         for g in group:
-            getattr(g, what)()
+            getattr(g, what)(*args)
+
+    def pass_on(h):
+        for group in second[h]:
+            run(group, "forward")
 
     for h in range(parts):
         arrive(h)
-        run(first[h], "forward")
-        if h:
-            run(second[h - 1], "forward")
-        run(first[h], "finish")
-        run(second[h], "start")
+        for n in range(3):
+            run(first[h], "take", n)
+            run(second[h][n + 1], "start")
+        if 0 < h < parts - 1:
+            pass_on(h - 1)
 
     total = 256
     pre = jnp.zeros((total, 256), F32)
     d_hidden = jnp.zeros((total, 128), F32)
-    start = 0
+    for load in loads:
+        load.wait()
     for h in range(parts):
-        if h == parts - 1:
-            run(second[h], "forward")
-        run(second[h], "finish")
-        if h == 0:
-            for load in loads:
-                load.wait()
+        if h >= max(parts - 2, 0) or parts == 1:
+            pass_on(h)
+        for group in second[h]:
+            run(group, "finish")
         width = cuts[h]
+        start = sum(cuts[:h])
         pre = pre + dot(gx[h][...].reshape(total, width), wcat[start : start + width, :])
         d_hidden = d_hidden + dot(gc[h][...].reshape(total, width), wd[start : start + width, :])
-        start += width
 
     gate_pre = pre[:, 0:128]
     up1 = pre[:, 128:256] + 1.0
@@ -217,15 +244,17 @@
     for q in range(4):
         part = dot(dcat, wcat[quarter * q : quarter * (q + 1), :], NT)
         for n in range(4):
-            pu[n, q] = part[64 * n : 64 * n + 32, :].astype(BF16)
-            pv[n, q] = part[64 * n + 32 : 64 * n + 64, :].astype(BF16)
+            for k in range(2):
+                at = 64 * n + 16 * k
+                pu[k, n, q] = part[at : at + 16, :].astype(BF16)
+                pv[k, n, q] = part[at + 32 : at + 48, :].astype(BF16)
 
     class Scatter:
-        def __init__(self, view, land, me, axis, ends, a, phase):
+        def __init__(self, view, land, me, axis, ends, k, a, phase):
             self.view, self.land, self.me, self.axis = view, land, me, axis
             self.ahead, self.behind, self.opposite = ends
-            self.ss = [rss.at[a, phase, n] for n in range(3)]
-            self.rs = [rsr.at[a, phase, n] for n in range(3)]
+            self.ss = [rss.at[k, a, phase, n] for n in range(3)]
+            self.rs = [rsr.at[k, a, phase, n] for n in range(3)]
 
         def copy(self, at, n, to):
             return pltpu.make_async_remote_copy(
@@ -252,64 +281,80 @@
             for n in range(3):
                 wait(self.land.at[n], self.ss[n])
 
-    u1 = Scatter(lambda n: pu.at[n], ru, x, "dp", xends, 0, 0)
-    v1 = Scatter(lambda n: pv.at[:, n], rv, y, "helper", yends, 1, 0)
-    u2 = Scatter(lambda n: qu.at[n], su, y, "helper", yends, 0, 1)
-    v2 = Scatter(lambda n: qv.at[n], sv, x, "dp", xends, 1, 1)
-    u1.start()
-    v1.start()
-
-    def weight_grads(h):
-        begin = sum(cuts[:h])
-        width = cuts[h]
-        both = dot(gx[h][...].reshape(total, width), dcat, TN).astype(BF16)
-        gg[begin : begin + width, :] = both[:, 0:128]
-        gu[begin : begin + width, :] = both[:, 128:256]
-        gd[begin : begin + width, :] = dot(gc[h][...].reshape(total, width), hidden, TN).astype(BF16)
-
-    weight_grads(0)
-    u1.forward()
-    v1.forward()
-    for h in range(1, parts):
-        weight_grads(h)
-    stores = [
-        pltpu.make_async_copy(gg, gg_hbm, osem.at[0]),
-        pltpu.make_async_copy(gu, gu_hbm, osem.at[1]),
-        pltpu.make_async_copy(gd, gd_hbm, osem.at[2]),
-    ]
-    for store in stores:
-        store.start()
-    qu[...] = u1.finish().astype(BF16)
-    u2.start()
-    qv[...] = v1.finish().astype(BF16)
-    v2.start()
-    u2.forward()
-    v2.forward()
-
-    back[0:32, :] = u2.finish()
-    back[32:64, :] = v2.finish()
-    for m in range(32):
-        ts[m] = back[2 * m : 2 * m + 2, :].astype(BF16)
-    for plane in range(4):
+    class DirectScatter(Scatter):
+        def start(self):
+            for n, to in enumerate((self.ahead, self.behind, self.opposite)):
+                self.copy(to, n, to).start()
+
+        def finish(self):
+            for n in range(3):
+                wait(self.land.at[n], self.rs[n])
+            terms = [self.land[n].astype(F32) for n in range(3)]
+            return self.view(self.me)[...].astype(F32) + terms[0] + terms[1] + terms[2]
+
+    one = [
+        (Scatter(lambda n, k=k: pu.at[k, n], ru.at[k], x, "dp", xends, k, 0, 0),
+         Scatter(lambda n, k=k: pv.at[k, :, n], rv.at[k], y, "helper", yends, k, 1, 0))
+        for k in range(2)
+    ]
+    two = [
+        (DirectScatter(lambda n, k=k: qu.at[k, n], su.at[k], y, "helper", yends, k, 0, 1),
+         DirectScatter(lambda n, k=k: qv.at[k, n], sv.at[k], x, "dp", xends, k, 1, 1))
+        for k in range(2)
+    ]
+    for k in range(2):
+        run(one[k], "start")
+
+    def weight_grads(h, begin, end):
+        cut = slice(begin, end)
+        both = dot(gx[h][:, :, :, cut].reshape(total, end - begin), dcat, TN).astype(BF16)
+        gg[cut, :] = both[:, 0:128]
+        gu[cut, :] = both[:, 128:256]
+        gd[cut, :] = dot(gc[h][:, :, :, cut].reshape(total, end - begin), hidden, TN).astype(BF16)
+
+    def give_back(plane, rows):
+        back[16 * plane : 16 * plane + 16, :] = rows
         for i in range(4):
             to = (z - shift(i, plane) + nz) % nz
             for core in range(2):
                 base = (plane * 4 + i) * 2
+                m = base + core
+                ts[m] = back[2 * m : 2 * m + 2, :].astype(BF16)
                 far = pltpu.make_async_remote_copy(
-                    ts.at[base + core], tr.at[base + c], ts_sem, tr_sem,
+                    ts.at[m], tr.at[base + c], ts_sem, tr_sem,
                     device_id={"expert": to * 2 + core}, device_id_type=MESH,
                 )
                 if shift(i, plane) == 0:
 
                     @pl.when(c == core)
                     def _():
-                        pltpu.make_async_copy(ts.at[base + core], tr.at[base + c], tr_sem).start()
+                        pltpu.make_async_copy(ts.at[m], tr.at[base + c], tr_sem).start()
 
                     @pl.when(c != core)
                     def _():
                         far.start()
                 else:
                     far.start()
+
+    weight_grads(0, 0, 1536)
+    run(one[0], "forward")
+    run(one[1], "forward")
+    weight_grads(0, 1536, model)
+    for k in range(2):
+        qu[k] = one[k][0].finish().astype(BF16)
+        two[k][0].start()
+        qv[k] = one[k][1].finish().astype(BF16)
+        two[k][1].start()
+    for k in range(2):
+        give_back(k, two[k][0].finish())
+        give_back(2 + k, two[k][1].finish())
+    stores = [
+        pltpu.make_async_copy(gg, gg_hbm, osem.at[0]),
+        pltpu.make_async_copy(gu, gu_hbm, osem.at[1]),
+        pltpu.make_async_copy(gd, gd_hbm, osem.at[2]),
+    ]
+    for store in stores:
+        store.start()
 
     r = lax.broadcasted_iota(jnp.int32, (64, 1), 0)
     home, _ = pick(idt, gvt, z, nz, (r // 4) % 4, r // 16, (r // 2) % 2, r % 2)
@@ -319,7 +364,6 @@
     gi_ref[...] = dot(home.astype(BF16), back[...].astype(BF16), TN).astype(BF16)
 
     for h in range(parts):
-
         @pl.when(y == 0)
         def _():
             wait(sb[h].at[0:7], zs.at[h])
@@ -329,10 +373,25 @@
             wait(sb[h], zs.at[h])
 
         run(first[h], "sent")
-        run(second[h], "sent")
-    for s in (u1, v1, u2, v2):
-        s.sent()
+        for group in second[h]:
+            run(group, "sent")
+    for k in range(2):
+        run(one[k], "sent")
+        run(two[k], "sent")
     wait(ts.at[0:31], ts_sem)
+    for store in stores:
+        store.wait()
+
+
+def hand_over(*refs):
+    ins, outs, held, sems = refs[0:4], refs[4:8], refs[8:12], refs[12]
+    loads = [pltpu.make_async_copy(ins[n], held[n], sems.at[0, n]) for n in range(4)]
+    stores = [pltpu.make_async_copy(held[n], outs[n], sems.at[1, n]) for n in range(4)]
+    for load in loads:
+        load.start()
+    for load, store in zip(loads, stores):
+        load.wait()
+        store.start()
     for store in stores:
         store.wait()
 
@@ -342,7 +401,7 @@
     nz = lax.axis_size("expert") // 2
     hidden = w_gate.shape[2]
     quarter = model // 4
-    cuts = (1536, model - 1536)
+    cuts = (model,)
     vmem = pl.BlockSpec(memory_space=pltpu.VMEM)
     anywhere = pl.BlockSpec(memory_space=pl.ANY)
     scratch = [pltpu.VMEM((8, 4, w), BF16) for w in cuts]
@@ -350,39 +409,44 @@
     scratch += [pltpu.VMEM((4, 4, 16, w), BF16) for w in cuts]
     scratch += [pltpu.VMEM((4, 4, 16, w), BF16) for w in cuts]
     scratch += [
+        pltpu.VMEM((tokens, model), BF16),
+        pltpu.VMEM((tokens, model), BF16),
+        pltpu.VMEM(expert_ids.shape[::-1], expert_ids.dtype),
+        pltpu.VMEM(gate_values.shape[::-1], gate_values.dtype),
         pltpu.VMEM((model, 2 * hidden), BF16),
         pltpu.VMEM((model, hidden), BF16),
         pltpu.VMEM((model, hidden), BF16),
         pltpu.VMEM((model, hidden), BF16),
         pltpu.VMEM((model, hidden), BF16),
         pltpu.VMEM((32, max(cuts)), F32),
-        pltpu.VMEM((4, 4, 32, quarter), BF16),
-        pltpu.VMEM((4, 4, 32, quarter), BF16),
-        pltpu.VMEM((3, 4, 32, quarter), BF16),
-        pltpu.VMEM((3, 4, 32, quarter), BF16),
-        pltpu.VMEM((4, 32, quarter), BF16),
-        pltpu.VMEM((4, 32, quarter), BF16),
-        pltpu.VMEM((3, 32, quarter), BF16),
-        pltpu.VMEM((3, 32, quarter), BF16),
+        pltpu.VMEM((2, 4, 4, 16, quarter), BF16),
+        pltpu.VMEM((2, 4, 4, 16, quarter), BF16),
+        pltpu.VMEM((2, 3, 4, 16, quarter), BF16),
+        pltpu.VMEM((2, 3, 4, 16, quarter), BF16),
+        pltpu.VMEM((2, 4, 16, quarter), BF16),
+        pltpu.VMEM((2, 4, 16, quarter), BF16),
+        pltpu.VMEM((2, 3, 16, quarter), BF16),
+        pltpu.VMEM((2, 3, 16, quarter), BF16),
         pltpu.VMEM((64, quarter), F32),
         pltpu.VMEM((32, 2, quarter), BF16),
         pltpu.VMEM((32, 2, quarter), BF16),
         pltpu.SemaphoreType.DMA((len(cuts),)),
         pltpu.SemaphoreType.DMA((len(cuts),)),
-        pltpu.SemaphoreType.DMA((len(cuts), 2, 2, 3)),
-        pltpu.SemaphoreType.DMA((len(cuts), 2, 2, 3)),
-        pltpu.SemaphoreType.DMA((2, 2, 3)),
-        pltpu.SemaphoreType.DMA((2, 2, 3)),
+        pltpu.SemaphoreType.DMA((len(cuts), 2, 5, 3)),
+        pltpu.SemaphoreType.DMA((len(cuts), 2, 5, 3)),
+        pltpu.SemaphoreType.DMA((2, 2, 2, 3)),
+        pltpu.SemaphoreType.DMA((2, 2, 2, 3)),
         pltpu.SemaphoreType.DMA,
         pltpu.SemaphoreType.DMA,
+        pltpu.SemaphoreType.DMA((4,)),
         pltpu.SemaphoreType.DMA((3,)),
         pltpu.SemaphoreType.DMA((3,)),
     ]
     grad = jax.ShapeDtypeStruct((model, hidden), BF16)
-    gi, gg, gu, gd = pl.pallas_call(
+    grads = pl.pallas_call(
         functools.partial(body, cuts, nz),
         out_shape=(jax.ShapeDtypeStruct((tokens, quarter), BF16), grad, grad, grad),
-        in_specs=[vmem] * 4 + [anywhere] * 3,
+        in_specs=[anywhere] * 7,
         out_specs=(vmem, anywhere, anywhere, anywhere),
         scratch_shapes=scratch,
         compiler_params=pltpu.CompilerParams(
@@ -397,6 +461,13 @@
         w_up[0],
         w_down[0].T,
     )
+    gi, gg, gu, gd = pl.pallas_call(
+        hand_over,
+        out_shape=tuple(jax.ShapeDtypeStruct(g.shape, g.dtype) for g in grads),
+        in_specs=[anywhere] * 4,
+        out_specs=(anywhere,) * 4,
+        scratch_shapes=[pltpu.VMEM(g.shape, g.dtype) for g in grads] + [pltpu.SemaphoreType.DMA((2, 4))],
+    )(*grads)
     return gi, gg[None], gu[None], gd.T[None]
 
 

time: 93.7 us -> 76.9 us (0.82)
  Pallas kernels: 87 us -> 76.1 us
  local copies, waits for them, and re-layouts: 5.69 us -> 0 us
    pallas_call x1, Pallas kernels: 87 us -> 73.5 us  [local(): pl.pallas_call(functools.partial(body, cuts, nz), out_shape=(jax.ShapeDty...]
    unnamed x8 -> x0, local copies, waits for them, and re-layouts: 5.69 us -> none
    pallas_call x0 -> x1, Pallas kernels: none -> 2.55 us  [local(): pl.pallas_call(hand_over, out_shape=tuple((jax.ShapeDtypeStruct(g.shape,...]
where the time goes in v2:
time: 76.9 us; the launch traced here: 76.7 us
  Pallas kernels  76.1 us (99%)
    pallas_call x1, Pallas kernels, local(): pl.pallas_call(functools.partial(body, cuts, nz), out_shape=(jax.ShapeDty...  73.5 us
    pallas_call x1, Pallas kernels, local(): pl.pallas_call(hand_over, out_shape=tuple((jax.ShapeDtypeStruct(g.shape,...  2.55 us

profile of v2, /device:TPU:1, one launch (start us, length us, event | category | flops | bytes accessed | tf_op | source)
XLA Modules:
  0.0 76.7 jit_solution(2883362564681764612)
XLA Ops:
  0.6 73.5 %shard_map.102 = (bf16[12,720]{1,0:T(8,128)(2,1)}, bf16[2880,128]{1,0:T(8,128)(2,1)}, bf16[2880,128]{1,0:T(8,128)(2,1)}, bf16[2880,128]{1,0:T(8,128)(2,1)}) custom-call(bf16[12,2880]{1,0:T(8,128)(2,1)} %x_hbm.1, bf16[12,2880]{1,0:T(8,128)(2,1)} %c_hbm.1, s32[4,12]{1,0:T(4,128)} %bitcast.15, f32[4,12]{1,0:T(4,128)} %bitcast.16, bf16[2880,128]{1,0:T(8,128)(2,1)} %bitcast.12, ...), custom_call_target="tpu_custom_call" | custom-call | tf_op jit(solution)/shard_map/pallas_call | solution.py:446
  74.2 2.6 %shard_map.103 = (bf16[12,720]{1,0:T(8,128)(2,1)}, bf16[2880,128]{1,0:T(8,128)(2,1)}, bf16[2880,128]{1,0:T(8,128)(2,1)}, bf16[2880,128]{1,0:T(8,128)(2,1)}) custom-call(bf16[12,720]{1,0:T(8,128)(2,1)} %get-tuple-element.12.refs_0_, bf16[2880,128]{1,0:T(8,128)(2,1)} %get-tuple-element.13.refs_1_, bf16[2880,128]{1,0:T(8,128)(2,1)} %get-tuple-element.14.refs_2_, ...), custom_call_target="tpu_custom_call" | custom-call | tf_op jit(solution)/shard_map/pallas_call | solution.py:464

commit v3 on v2

--- a/solution.py
+++ b/solution.py
@@ -43,11 +43,11 @@
     return chosen, jnp.sum(chosen * weight, axis=1, keepdims=True)
 
 
-def body(cuts, nz, x_hbm, c_hbm, idt_hbm, gvt_hbm, wg_hbm, wu_hbm, wd_hbm, gi_ref, gg_hbm, gu_hbm, gd_hbm, *rest):
+def body(cuts, nz, x_hbm, c_hbm, idt_hbm, gvt_hbm, wg_hbm, wu_hbm, wd_hbm, gi_ref, gg, gu, gd, *rest):
     parts = len(cuts)
     sb, rb, gx, gc = (rest[n * parts : (n + 1) * parts] for n in range(4))
-    (x_ref, c_ref, idt_ref, gvt_ref, wcat, wd, gg, gu, gd, stage, pu, pv, ru, rv, qu, qv, su, sv, back, ts, tr,
-     zs, zr, ags, agr, rss, rsr, ts_sem, tr_sem, isem, wsem, osem) = rest[4 * parts :]
+    (x_ref, c_ref, idt_ref, gvt_ref, wcat, wd, stage, pu, pv, ru, rv, qu, qv, su, sv, back, ts, tr,
+     zs, zr, ags, agr, rss, rsr, ts_sem, tr_sem, isem, wsem) = rest[4 * parts :]
     e = lax.axis_index("expert")
     y = lax.axis_index("helper")
     x = lax.axis_index("dp")
@@ -65,8 +65,7 @@
 
     barrier = pltpu.get_barrier_semaphore()
 
-    @pl.loop(1, ne)
-    def _(n):
+    for n in sorted(range(1, ne), key=lambda n: -min(n, ne - n)):
         pl.semaphore_signal(barrier, inc=1, device_id={"expert": (e + n) % ne}, device_id_type=MESH)
 
     for other in (xa, xb, xo):
@@ -314,7 +313,7 @@
 
     def give_back(plane, rows):
         back[16 * plane : 16 * plane + 16, :] = rows
-        for i in range(4):
+        for i in (1, 3, 0, 2):
             to = (z - shift(i, plane) + nz) % nz
             for core in range(2):
                 base = (plane * 4 + i) * 2
@@ -336,10 +335,8 @@
                 else:
                     far.start()
 
-    weight_grads(0, 0, 1536)
     run(one[0], "forward")
     run(one[1], "forward")
-    weight_grads(0, 1536, model)
     for k in range(2):
         qu[k] = one[k][0].finish().astype(BF16)
         two[k][0].start()
@@ -348,14 +345,7 @@
     for k in range(2):
         give_back(k, two[k][0].finish())
         give_back(2 + k, two[k][1].finish())
-    stores = [
-        pltpu.make_async_copy(gg, gg_hbm, osem.at[0]),
-        pltpu.make_async_copy(gu, gu_hbm, osem.at[1]),
-        pltpu.make_async_copy(gd, gd_hbm, osem.at[2]),
-    ]
-    for store in stores:
-        store.start()
-
+    weight_grads(0, 0, model)
     r = lax.broadcasted_iota(jnp.int32, (64, 1), 0)
     home, _ = pick(idt, gvt, z, nz, (r // 4) % 4, r // 16, (r // 2) % 2, r % 2)
     wait(tr, tr_sem)
@@ -379,21 +369,14 @@
         run(one[k], "sent")
         run(two[k], "sent")
     wait(ts.at[0:31], ts_sem)
-    for store in stores:
-        store.wait()
 
 
 def hand_over(*refs):
-    ins, outs, held, sems = refs[0:4], refs[4:8], refs[8:12], refs[12]
-    loads = [pltpu.make_async_copy(ins[n], held[n], sems.at[0, n]) for n in range(4)]
-    stores = [pltpu.make_async_copy(held[n], outs[n], sems.at[1, n]) for n in range(4)]
-    for load in loads:
-        load.start()
-    for load, store in zip(loads, stores):
-        load.wait()
-        store.start()
-    for store in stores:
-        store.wait()
+    copies = [pltpu.make_async_copy(refs[n], refs[4 + n], refs[8].at[n]) for n in range(4)]
+    for copy in copies:
+        copy.start()
+    for copy in copies:
+        copy.wait()
 
 
 def local(inputs, cotangent, expert_ids, gate_values, w_gate, w_up, w_down):
@@ -414,9 +397,6 @@
         pltpu.VMEM(expert_ids.shape[::-1], expert_ids.dtype),
         pltpu.VMEM(gate_values.shape[::-1], gate_values.dtype),
         pltpu.VMEM((model, 2 * hidden), BF16),
-        pltpu.VMEM((model, hidden), BF16),
-        pltpu.VMEM((model, hidden), BF16),
-        pltpu.VMEM((model, hidden), BF16),
         pltpu.VMEM((model, hidden), BF16),
         pltpu.VMEM((32, max(cuts)), F32),
         pltpu.VMEM((2, 4, 4, 16, quarter), BF16),
@@ -440,14 +420,13 @@
         pltpu.SemaphoreType.DMA,
         pltpu.SemaphoreType.DMA((4,)),
         pltpu.SemaphoreType.DMA((3,)),
-        pltpu.SemaphoreType.DMA((3,)),
-    ]
-    grad = jax.ShapeDtypeStruct((model, hidden), BF16)
+    ]
+    grad = pltpu.VMEM((model, hidden), BF16)
     grads = pl.pallas_call(
         functools.partial(body, cuts, nz),
-        out_shape=(jax.ShapeDtypeStruct((tokens, quarter), BF16), grad, grad, grad),
+        out_shape=(pltpu.VMEM((tokens, quarter), BF16), grad, grad, grad),
         in_specs=[anywhere] * 7,
-        out_specs=(vmem, anywhere, anywhere, anywhere),
+        out_specs=(vmem,) * 4,
         scratch_shapes=scratch,
         compiler_params=pltpu.CompilerParams(
             collective_id=0, has_side_effects=True, vmem_limit_bytes=56 * 1024 * 1024
@@ -466,8 +445,8 @@
         out_shape=tuple(jax.ShapeDtypeStruct(g.shape, g.dtype) for g in grads),
         in_specs=[anywhere] * 4,
         out_specs=(anywhere,) * 4,
-        scratch_shapes=[pltpu.VMEM(g.shape, g.dtype) for g in grads] + [pltpu.SemaphoreType.DMA((2, 4))],
-    )(*grads)
+        scratch_shapes=[pltpu.SemaphoreType.DMA((4,))],
+    )(*(pltpu.with_memory_space_constraint(g, pltpu.VMEM) for g in grads))
     return gi, gg[None], gu[None], gd.T[None]
 
 

time: 76.9 us -> 74.6 us (0.970)
  Pallas kernels: 76.1 us -> 73.8 us
    pallas_call x1, Pallas kernels: 2.55 us -> 1.39 us  [local(): pl.pallas_call(hand_over, out_shape=tuple((jax.ShapeDtypeStruct(g.shape,...]
    pallas_call x1, Pallas kernels: 73.5 us -> 72.4 us  [local(): pl.pallas_call(functools.partial(body, cuts, nz), out_shape=(pltpu.VMEM((...]
where the time goes in v3:
time: 74.6 us; the launch traced here: 74.4 us
  Pallas kernels  73.8 us (99%)
    pallas_call x1, Pallas kernels, local(): pl.pallas_call(functools.partial(body, cuts, nz), out_shape=(pltpu.VMEM((...  72.4 us

profile of v3, /device:TPU:1, one launch (start us, length us, event | category | flops | bytes accessed | tf_op | source)
XLA Modules:
  0.0 74.4 jit_solution(16547726860518541625)
XLA Ops:
  0.6 72.4 %shard_map.102 = (bf16[12,720]{1,0:T(8,128)(2,1)S(1)}, bf16[2880,128]{1,0:T(8,128)(2,1)S(1)}, bf16[2880,128]{1,0:T(8,128)(2,1)S(1)}, bf16[2880,128]{1,0:T(8,128)(2,1)S(1)}) custom-call(bf16[12,2880]{1,0:T(8,128)(2,1)} %x_hbm.1, bf16[12,2880]{1,0:T(8,128)(2,1)} %c_hbm.1, s32[4,12]{1,0:T(4,128)} %bitcast.15, f32[4,12]{1,0:T(4,128)} %bitcast.16, ...), custom_call_target="tpu_custom_call" | custom-call | tf_op jit(solution)/shard_map/pallas_call | solution.py:425
  73.0 1.4 %shard_map.103 = (bf16[12,720]{1,0:T(8,128)(2,1)}, bf16[2880,128]{1,0:T(8,128)(2,1)}, bf16[2880,128]{1,0:T(8,128)(2,1)}, bf16[2880,128]{1,0:T(8,128)(2,1)}) custom-call(bf16[12,720]{1,0:T(8,128)(2,1)S(1)} %get-tuple-element.12.refs_0_, bf16[2880,128]{1,0:T(8,128)(2,1)S(1)} %get-tuple-element.13.refs_1_, bf16[2880,128]{1,0:T(8,128)(2,1)S(1)} %get-tuple-element.14.refs_2_, ...), custom_call_target="tpu_custom_call" | custom-call | tf_op jit(solution)/shard_map/pallas_call | solution.py:443

commit v4 on v3

--- a/solution.py
+++ b/solution.py
@@ -21,11 +21,13 @@
 
 
 def shift(i, y):
-    return (1 + y, 8 - y, -y, y - 7)[i]
+    none = 1 - (y + 3) // 4
+    return (y + 4 * none, -y - 4 * none, 8 - y, (y - 8) * (1 - none))[i]
 
 
 def pick_shift(i, y):
-    return jnp.where(i == 0, 1 + y, jnp.where(i == 1, 8 - y, jnp.where(i == 2, -y, y - 7)))
+    a, b, c, d = (shift(n, y) for n in range(4))
+    return jnp.where(i == 0, a, jnp.where(i == 1, b, jnp.where(i == 2, c, d)))
 
 
 def pick(idt, gvt, z, nz, i, y, core, j):
@@ -111,7 +113,7 @@
         pltpu.make_async_copy(ref, ref, sem).wait()
 
     for h in range(parts):
-        for i in (1, 3, 0, 2):
+        for i in (2, 3, 0, 1):
             to = (z + shift(i, y) + nz) % nz
             for core in range(2):
                 s = 2 * i + core
@@ -119,7 +121,7 @@
                     sb[h].at[s], rb[h].at[2 * i + c], zs.at[h], zr.at[h],
                     device_id={"expert": to * 2 + core}, device_id_type=MESH,
                 )
-                if i == 2:
+                if i == 3:
                     own = (y == 0) & (c == core)
 
                     @pl.when(own)
@@ -313,7 +315,7 @@
 
     def give_back(plane, rows):
         back[16 * plane : 16 * plane + 16, :] = rows
-        for i in (1, 3, 0, 2):
+        for i in (2, 3, 0, 1):
             to = (z - shift(i, plane) + nz) % nz
             for core in range(2):
                 base = (plane * 4 + i) * 2

time: 74.6 us -> 73.4 us (0.984)
  Pallas kernels: 73.8 us -> 72.6 us
    pallas_call x1, Pallas kernels: 72.4 us -> 71.2 us  [local(): pl.pallas_call(functools.partial(body, cuts, nz), out_shape=(pltpu.VMEM((...]
where the time goes in v4:
time: 73.4 us; the launch traced here: 73.2 us
  Pallas kernels  72.6 us (99%)
    pallas_call x1, Pallas kernels, local(): pl.pallas_call(functools.partial(body, cuts, nz), out_shape=(pltpu.VMEM((...  71.2 us

profile of v4, /device:TPU:1, one launch (start us, length us, event | category | flops | bytes accessed | tf_op | source)
XLA Modules:
  0.0 73.2 jit_solution(10053990616849151552)
XLA Ops:
  0.6 71.2 %shard_map.102 = (bf16[12,720]{1,0:T(8,128)(2,1)S(1)}, bf16[2880,128]{1,0:T(8,128)(2,1)S(1)}, bf16[2880,128]{1,0:T(8,128)(2,1)S(1)}, bf16[2880,128]{1,0:T(8,128)(2,1)S(1)}) custom-call(bf16[12,2880]{1,0:T(8,128)(2,1)} %x_hbm.1, bf16[12,2880]{1,0:T(8,128)(2,1)} %c_hbm.1, s32[4,12]{1,0:T(4,128)} %bitcast.15, f32[4,12]{1,0:T(4,128)} %bitcast.16, ...), custom_call_target="tpu_custom_call" | custom-call | tf_op jit(solution)/shard_map/pallas_call | solution.py:427
  71.8 1.4 %shard_map.103 = (bf16[12,720]{1,0:T(8,128)(2,1)}, bf16[2880,128]{1,0:T(8,128)(2,1)}, bf16[2880,128]{1,0:T(8,128)(2,1)}, bf16[2880,128]{1,0:T(8,128)(2,1)}) custom-call(bf16[12,720]{1,0:T(8,128)(2,1)S(1)} %get-tuple-element.12.refs_0_, bf16[2880,128]{1,0:T(8,128)(2,1)S(1)} %get-tuple-element.13.refs_1_, bf16[2880,128]{1,0:T(8,128)(2,1)S(1)} %get-tuple-element.14.refs_2_, ...), custom_call_target="tpu_custom_call" | custom-call | tf_op jit(solution)/shard_map/pallas_call | solution.py:445

commit v5 on v4

--- a/solution.py
+++ b/solution.py
@@ -155,31 +155,25 @@
             wait(self.view(self.behind), self.rs[0])
             self.copy(self.behind, 2, self.ahead).start()
 
+        def take(self, n):
+            if n == 0:
+                self.forward()
+            else:
+                wait(self.view((self.ahead, self.opposite)[n - 1]), self.rs[n])
+
         def finish(self):
-            wait(self.view(self.ahead), self.rs[1])
-            wait(self.view(self.opposite), self.rs[2])
+            self.take(1)
+            self.take(2)
 
         def sent(self):
             wait(self.view(self.me), self.ss[0])
             wait(self.view(self.me), self.ss[1])
             wait(self.view(self.behind), self.ss[2])
 
-    class Direct(Gather):
-        def start(self):
-            for n, to in enumerate((self.ahead, self.behind, self.opposite)):
-                self.copy(self.me, n, to).start()
-
-        def take(self, n):
-            wait(self.view((self.behind, self.ahead, self.opposite)[n]), self.rs[n])
-
-        def sent(self):
-            for n in range(3):
-                wait(self.view(self.me), self.ss[n])
-
     xends, yends = (xa, xb, xo), (ya, yb, yo)
     first = [
-        (Direct(lambda n, h=h: gx[h].at[n, y], x, "dp", xends, h, 0, 4),
-         Direct(lambda n, h=h: gc[h].at[x, n], y, "helper", yends, h, 1, 4))
+        (Gather(lambda n, h=h: gx[h].at[n, y], x, "dp", xends, h, 0, 4),
+         Gather(lambda n, h=h: gc[h].at[x, n], y, "helper", yends, h, 1, 4))
         for h in range(parts)
     ]
     xroles, yroles = (x, xb, xa, xo), (y, yb, ya, yo)
@@ -193,13 +187,11 @@
     def arrive(h):
         wait(rb[h], zr.at[h])
         width = cuts[h]
-        for s in range(8):
-            rows = rb[h][s].astype(F32)
-            stage[2 * s : 2 * s + 2, 0:width] = rows[0:2]
-            stage[16 + 2 * s : 18 + 2 * s, 0:width] = rows[2:4]
-        gx[h][x, y] = stage[0:16, 0:width].astype(BF16)
-        gc[h][x, y] = stage[16:32, 0:width].astype(BF16)
-        run(first[h], "start")
+        for a, there in enumerate((gx, gc)):
+            for s in range(8):
+                stage[2 * s : 2 * s + 2, 0:width] = rb[h][s].astype(F32)[2 * a : 2 * a + 2]
+            there[h][x, y] = stage[0:16, 0:width].astype(BF16)
+            first[h][a].start()
         run(second[h][0], "start")
 
     def run(group, what, *args):
@@ -265,6 +257,8 @@
 
         def start(self):
             self.copy(self.opposite, 0, self.ahead).start()
+
+        def start_last(self):
             self.copy(self.behind, 1, self.behind).start()
 
         def forward(self):
@@ -284,7 +278,7 @@
 
     class DirectScatter(Scatter):
         def start(self):
-            for n, to in enumerate((self.ahead, self.behind, self.opposite)):
+            for n, to in ((2, self.opposite), (0, self.ahead), (1, self.behind)):
                 self.copy(to, n, to).start()
 
         def finish(self):
@@ -305,6 +299,8 @@
     ]
     for k in range(2):
         run(one[k], "start")
+    for k in range(2):
+        run(one[k], "start_last")
 
     def weight_grads(h, begin, end):
         cut = slice(begin, end)

time: 73.4 us -> 73 us (level)
  no operation moved by 1% of the time
where the time goes in v5:
time: 73 us; the launch traced here: 72.9 us
  Pallas kernels  72.2 us (99%)
    pallas_call x1, Pallas kernels, local(): pl.pallas_call(functools.partial(body, cuts, nz), out_shape=(pltpu.VMEM((...  70.9 us

profile of v5, /device:TPU:1, one launch (start us, length us, event | category | flops | bytes accessed | tf_op | source)
XLA Modules:
  0.0 72.9 jit_solution(9396032866106399670)
XLA Ops:
  0.6 70.9 %shard_map.102 = (bf16[12,720]{1,0:T(8,128)(2,1)S(1)}, bf16[2880,128]{1,0:T(8,128)(2,1)S(1)}, bf16[2880,128]{1,0:T(8,128)(2,1)S(1)}, bf16[2880,128]{1,0:T(8,128)(2,1)S(1)}) custom-call(bf16[12,2880]{1,0:T(8,128)(2,1)} %x_hbm.1, bf16[12,2880]{1,0:T(8,128)(2,1)} %c_hbm.1, s32[4,12]{1,0:T(4,128)} %bitcast.15, f32[4,12]{1,0:T(4,128)} %bitcast.16, ...), custom_call_target="tpu_custom_call" | custom-call | tf_op jit(solution)/shard_map/pallas_call | solution.py:423
  71.5 1.4 %shard_map.103 = (bf16[12,720]{1,0:T(8,128)(2,1)}, bf16[2880,128]{1,0:T(8,128)(2,1)}, bf16[2880,128]{1,0:T(8,128)(2,1)}, bf16[2880,128]{1,0:T(8,128)(2,1)}) custom-call(bf16[12,720]{1,0:T(8,128)(2,1)S(1)} %get-tuple-element.12.refs_0_, bf16[2880,128]{1,0:T(8,128)(2,1)S(1)} %get-tuple-element.13.refs_1_, bf16[2880,128]{1,0:T(8,128)(2,1)S(1)} %get-tuple-element.14.refs_2_, ...), custom_call_target="tpu_custom_call" | custom-call | tf_op jit(solution)/shard_map/pallas_call | solution.py:441
